TPU v7x, 32 devices: a whole 2x2x4 slice. The times are simulated.
32 devices in a mesh: dp: 16 (over z, y, x), tensor: 2 (over core).
Axes of the slice: x: 2, y: 2, z: 4, core: 2. Of those that a mesh axis runs over, the one named last changes fastest.
Arguments:
- tokens: bfloat16 [16384, 1024], P('dp'), may hold values from -6 to 6
- norm_gain: float32 [1024], replicated, may hold values from 0.5 to 1.5
- z_proj: bfloat16 [1024, 2048], P(None, 'tensor'), may hold values from -0.1875 to 0.1875
- x_proj: bfloat16 [1024, 2048], P(None, 'tensor'), may hold values from -0.1875 to 0.1875
- dt_proj: bfloat16 [1024, 32], P(None, 'tensor'), may hold values from -0.1875 to 0.1875
- bc_proj: bfloat16 [1024, 256], replicated, may hold values from -0.1875 to 0.1875
- x_conv: float32 [4, 2048], P(None, 'tensor'), may hold values from -1.5 to 1.5
- x_conv_bias: float32 [2048], P('tensor'), may hold values from -1 to 1
- bc_conv: float32 [4, 256], replicated, may hold values from -1.5 to 1.5
- bc_conv_bias: float32 [256], replicated, may hold values from -1 to 1
- dt_bias: float32 [32], P('tensor'), may hold values from -4.6 to -2.3
- a_log: float32 [32], P('tensor'), may hold values from 0 to 2.77
- d_skip: float32 [32], P('tensor'), may hold values from 0.5 to 1.5
- gate_gain: float32 [2048], P('tensor'), may hold values from 0.5 to 1.5
- out_proj: bfloat16 [2048, 1024], P('tensor'), may hold values from -0.125 to 0.125
- cotangent: bfloat16 [16384, 1024], P('dp'), may hold values from -6 to 6
Outputs:
- mixed: bfloat16 [16384, 1024], P('dp')
- tokens_grad: bfloat16 [16384, 1024], P('dp')
- norm_gain_grad: float32 [1024], replicated
- z_proj_grad: float32 [1024, 2048], P(None, 'tensor')
- x_proj_grad: float32 [1024, 2048], P(None, 'tensor')
- dt_proj_grad: float32 [1024, 32], P(None, 'tensor')
- bc_proj_grad: float32 [1024, 256], replicated
- x_conv_grad: float32 [4, 2048], P(None, 'tensor')
- x_conv_bias_grad: float32 [2048], P('tensor')
- bc_conv_grad: float32 [4, 256], replicated
- bc_conv_bias_grad: float32 [256], replicated
- dt_bias_grad: float32 [32], P('tensor')
- a_log_grad: float32 [32], P('tensor')
- d_skip_grad: float32 [32], P('tensor')
- gate_gain_grad: float32 [2048], P('tensor')
- out_proj_grad: float32 [2048, 1024], P('tensor')
All inputs are finite; a program needn't handle non-finite values.
Results may differ from a plain program's by a relative error of at most 0.02.
Values may be sent and summed in bfloat16 or wider, within the bound.
A program may use at most 128 MiB of HBM per device.

v0:
```python
import jax
import jax.numpy as jnp
from jax import lax
from jax.sharding import PartitionSpec as P

INNER = 2048
STRETCH = 256
SEQ_LEN = 1024


EPS = 1e-05
HIGH = lax.Precision.HIGHEST


def causal_conv(sequence, weights, offsets):
    row_count, channels = sequence.shape
    kernel_width = weights.shape[0]
    blocked = sequence.reshape(row_count // SEQ_LEN, SEQ_LEN, channels)
    padded = jnp.pad(blocked, ((0, 0), (kernel_width - 1, 0), (0, 0)))
    summed = jnp.zeros_like(blocked) + offsets
    for offset in range(kernel_width):
        summed = summed + weights[offset] * padded[:, offset : offset + SEQ_LEN]
    return jax.nn.silu(summed).reshape(row_count, channels)


def ssd_sequence(values, step_dt, decay_rates, input_b, output_c):
    length, head_count, head_dim = values.shape
    state_size = input_b.shape[1]
    block_count = length // STRETCH
    places = jnp.arange(STRETCH)
    lower_mask = (places[:, None] >= places[None, :])[:, :, None]

    def advance(inner_state, block_data):
        block_vals, block_dt, block_b, block_c = block_data
        cumulative = jnp.cumsum(block_dt * decay_rates, axis=0)
        spreads = jnp.where(lower_mask, cumulative[:, None, :] - cumulative[None, :, :], 0.0)
        decays = jnp.where(lower_mask, jnp.exp(spreads), 0.0)
        scores = jnp.dot(block_c, block_b.T, precision=HIGH)
        mixing = scores[:, :, None] * decays * block_dt[None, :, :]
        within = jnp.einsum("ijh,jhp->ihp", mixing, block_vals, precision=HIGH)
        carried = (
            jnp.einsum("in,hpn->ihp", block_c, inner_state, precision=HIGH)
            * jnp.exp(cumulative)[:, :, None]
        )
        tail_gain = jnp.exp(cumulative[-1][None, :] - cumulative) * block_dt
        arrival = jnp.einsum("jh,jn,jhp->hpn", tail_gain, block_b, block_vals, precision=HIGH)
        return (inner_state * jnp.exp(cumulative[-1])[:, None, None] + arrival, within + carried)

    initial = jnp.zeros((head_count, head_dim, state_size), jnp.float32)
    _, results = lax.scan(
        jax.checkpoint(advance),
        initial,
        (
            values.reshape(block_count, STRETCH, head_count, head_dim),
            step_dt.reshape(block_count, STRETCH, head_count),
            input_b.reshape(block_count, STRETCH, state_size),
            output_c.reshape(block_count, STRETCH, state_size),
        ),
    )
    return results.reshape(length, head_count, head_dim)


def mixer(
    z_pre, x_pre, dt_pre, bc_pre, x_conv, x_conv_bias, bc_conv, bc_conv_bias, dt_bias, a_log, d_skip
):
    row_count = z_pre.shape[0]
    head_count = dt_pre.shape[1]
    head_dim = x_pre.shape[1] // head_count
    x_mixed = causal_conv(x_pre, x_conv, x_conv_bias)
    bc_mixed = causal_conv(bc_pre, bc_conv, bc_conv_bias)
    state_size = bc_mixed.shape[1] // 2
    step_dt = jax.nn.softplus(dt_pre + dt_bias)
    decay_rates = -jnp.exp(a_log)
    seq_count = row_count // SEQ_LEN
    values = x_mixed.reshape(seq_count, SEQ_LEN, head_count, head_dim)
    scanned = jax.vmap(ssd_sequence, in_axes=(0, 0, None, 0, 0))(
        values,
        step_dt.reshape(seq_count, SEQ_LEN, head_count),
        decay_rates,
        bc_mixed[:, :state_size].reshape(seq_count, SEQ_LEN, state_size),
        bc_mixed[:, state_size:].reshape(seq_count, SEQ_LEN, state_size),
    )
    scanned = scanned + d_skip[:, None] * values
    return scanned.reshape(row_count, head_count * head_dim) * jax.nn.silu(z_pre)


def proj_back(grad_rows, weights):
    return lax.dot_general(
        grad_rows, weights, (((1,), (1,)), ((), ())), preferred_element_type=jnp.float32
    )


def over_rows(left, right):
    return lax.dot_general(
        left, right, (((0,), (0,)), ((), ())), preferred_element_type=jnp.float32
    )


def per_device(
    tokens,
    norm_gain,
    z_proj,
    x_proj,
    dt_proj,
    bc_proj,
    x_conv,
    x_conv_bias,
    bc_conv,
    bc_conv_bias,
    dt_bias,
    a_log,
    d_skip,
    gate_gain,
    out_proj,
    cotangent,
):
    row_count = tokens.shape[0]
    share_rows = row_count // lax.axis_size("tensor")
    share_start = lax.axis_index("tensor") * share_rows

    def take_rows(source, first_row, row_span):
        return lax.dynamic_slice_in_dim(source, first_row, row_span, 0)

    hidden = tokens.astype(jnp.float32)
    inv_rms = lax.rsqrt(jnp.mean(hidden * hidden, axis=1, keepdims=True) + EPS)
    normed = hidden * inv_rms
    normed_in = (normed * norm_gain).astype(jnp.bfloat16)
    z_pre = jnp.dot(normed_in, z_proj, preferred_element_type=jnp.float32)
    x_pre = jnp.dot(normed_in, x_proj, preferred_element_type=jnp.float32)
    dt_pre = jnp.dot(normed_in, dt_proj, preferred_element_type=jnp.float32)
    bc_pre = jnp.dot(normed_in, bc_proj, preferred_element_type=jnp.float32)
    gated, mixer_pull = jax.vjp(
        mixer,
        z_pre,
        x_pre,
        dt_pre,
        bc_pre,
        x_conv,
        x_conv_bias,
        bc_conv,
        bc_conv_bias,
        dt_bias,
        a_log,
        d_skip,
    )
    squares = lax.psum(jnp.sum(gated * gated, axis=1), "tensor")
    gate_rms = lax.rsqrt(squares / INNER + EPS)[:, None]
    gate_hat = gated * gate_rms
    gate_out = (gate_hat * gate_gain).astype(jnp.bfloat16)
    branch = lax.psum(
        jnp.dot(gate_out, out_proj, preferred_element_type=jnp.float32).astype(jnp.bfloat16),
        "tensor",
    ).astype(jnp.float32)
    mixed = (hidden + branch).astype(jnp.bfloat16)
    out_proj_grad = over_rows(gate_out, cotangent)
    gate_in_grad = proj_back(cotangent, out_proj)
    gate_gain_grad = jnp.sum(gate_in_grad * gate_hat, axis=0)
    hat_grad = gate_in_grad * gate_gain
    gate_stat = lax.psum(jnp.sum(hat_grad * gate_hat, axis=1), "tensor")
    gated_grad = gate_rms * (hat_grad - gate_hat * (gate_stat / INNER)[:, None])
    (
        z_grad,
        x_grad,
        dt_grad,
        bc_grad,
        x_conv_grad,
        x_conv_bias_grad,
        bc_conv_grad,
        bc_conv_bias_grad,
        dt_bias_grad,
        a_log_grad,
        d_skip_grad,
    ) = mixer_pull(gated_grad)
    z_low = z_grad.astype(jnp.bfloat16)
    x_low = x_grad.astype(jnp.bfloat16)
    dt_low = dt_grad.astype(jnp.bfloat16)
    bc_low = bc_grad.astype(jnp.bfloat16)
    normed_share = take_rows(normed, share_start, share_rows)
    summed = proj_back(take_rows(z_low, 0, row_count), z_proj)
    summed = summed + proj_back(take_rows(x_low, 0, row_count), x_proj)
    summed = summed + proj_back(take_rows(dt_low, 0, row_count), dt_proj)
    full_grad = lax.psum(
        (summed + proj_back(take_rows(bc_low, 0, row_count), bc_proj)).astype(jnp.bfloat16),
        "tensor",
    ).astype(jnp.float32)
    scaled = full_grad * norm_gain
    full_back = inv_rms * (scaled - normed * jnp.mean(scaled * normed, axis=1, keepdims=True))
    tokens_grad = (full_back + cotangent.astype(jnp.float32)).astype(jnp.bfloat16)
    normed_grad = take_rows(full_grad, share_start, share_rows)
    norm_gain_grad = jnp.sum(normed_grad * normed_share, axis=0)
    z_proj_grad = over_rows(normed_in, z_low)
    x_proj_grad = over_rows(normed_in, x_low)
    dt_proj_grad = over_rows(normed_in, dt_low)
    bc_proj_grad = over_rows(normed_in, bc_low)
    (
        z_proj_grad,
        x_proj_grad,
        dt_proj_grad,
        x_conv_grad,
        x_conv_bias_grad,
        dt_bias_grad,
        a_log_grad,
        d_skip_grad,
        gate_gain_grad,
        out_proj_grad,
    ) = (
        lax.psum(z_proj_grad.astype(jnp.bfloat16), "dp").astype(jnp.float32),
        lax.psum(x_proj_grad.astype(jnp.bfloat16), "dp").astype(jnp.float32),
        lax.psum(dt_proj_grad.astype(jnp.bfloat16), "dp").astype(jnp.float32),
        lax.psum(x_conv_grad.astype(jnp.bfloat16), "dp").astype(jnp.float32),
        lax.psum(x_conv_bias_grad.astype(jnp.bfloat16), "dp").astype(jnp.float32),
        lax.psum(dt_bias_grad.astype(jnp.bfloat16), "dp").astype(jnp.float32),
        lax.psum(a_log_grad.astype(jnp.bfloat16), "dp").astype(jnp.float32),
        lax.psum(d_skip_grad.astype(jnp.bfloat16), "dp").astype(jnp.float32),
        lax.psum(gate_gain_grad.astype(jnp.bfloat16), "dp").astype(jnp.float32),
        lax.psum(out_proj_grad.astype(jnp.bfloat16), "dp").astype(jnp.float32),
    )
    bc_proj_grad, bc_conv_grad, bc_conv_bias_grad, norm_gain_grad = lax.psum(
        (bc_proj_grad, bc_conv_grad, bc_conv_bias_grad, norm_gain_grad), ("dp", "tensor")
    )
    return (
        mixed,
        tokens_grad,
        norm_gain_grad,
        z_proj_grad,
        x_proj_grad,
        dt_proj_grad,
        bc_proj_grad,
        x_conv_grad,
        x_conv_bias_grad,
        bc_conv_grad,
        bc_conv_bias_grad,
        dt_bias_grad,
        a_log_grad,
        d_skip_grad,
        gate_gain_grad,
        out_proj_grad,
    )


def solution(mesh):
    placed = (
        P("dp", None),
        P(),
        P(None, "tensor"),
        P(None, "tensor"),
        P(None, "tensor"),
        P(),
        P(None, "tensor"),
        P("tensor"),
        P(),
        P(),
        P("tensor"),
        P("tensor"),
        P("tensor"),
        P("tensor"),
        P("tensor", None),
        P("dp", None),
    )
    return jax.shard_map(
        per_device,
        mesh=mesh,
        in_specs=placed,
        out_specs=(
            P("dp", None),
            P("dp", None),
            P(),
            P(None, "tensor"),
            P(None, "tensor"),
            P(None, "tensor"),
            P(),
            P(None, "tensor"),
            P("tensor"),
            P(),
            P(),
            P("tensor"),
            P("tensor"),
            P("tensor"),
            P("tensor"),
            P("tensor", None),
        ),
        check_vma=False,
    )
```

profile of v0, /device:TPU:0, one launch (start us, length us, event | category | flops | bytes accessed | tf_op | source)
XLA Modules:
  0.0 835.8 jit_solution(25478895712858171)
XLA Ops:
  10.4 4.2 convert_multiply_fusion
  22.5 4.8 fusion.136
  27.3 7.2 reshape.975
  34.5 7.7 copy.214
  42.3 2.9 compare_select_fusion.2
  48.3 61.0 %while.44 = (s32[]{:T(128)}, f32[1,16,64,128]{3,2,1,0:T(8,128)S(1)}, f32[4,1,256,16,64]{2,4,3,1,0:T(8,128)}, f32[4,1,16,64,128]{4,3,2,1,0:T(8,128)}, f32[4,1,256...) while((s32[]{:T(128)}, ...), condition=%wide.region_4.5_spmd.clone.clone, body=%wide.region_1.4_spmd.clone.clone.sunk | while | flops 1718497280 | bytes 9492249 | solution.py:50
  52.7 7.1 fusion.278
  68.0 7.1 fusion.278
  83.2 7.1 fusion.278
  98.5 7.1 fusion.278
  109.3 8.1 copy.235
  117.4 8.0 reshape.972
  125.5 9.1 %multiply_reduce_fusion.9 = (f32[1024]{0:T(1024)S(1)}, f32[1024,1024]{1,0:T(8,128)}, f32[1024,1024]{1,0:T(8,128)}) fusion(f32[1024,1024]{1,0:T(8,128)} %reshape.972, f32[1,1024,1024]{2,1,0:T(8,128)} %get-tuple-element.807, f32[1024]{0:T(1024)S(1)} %mul.773, bf16[1024,1024]{1,0:T(8,128)(2,1)} %copy-done.7, bf16[1024,1024]{1,0:T(8,128)(2,1)S(1)} %copy-done), kind=kOutput, calls=%fused_computation.202 | convolution fusion | flops 2161114112 | bytes 20979712 | tf_op jit(solution)/shard_map/dot_general | solution.py:128
  137.2 6.8 convolution_convert_fusion.3
  144.0 5.1 multiply_reduce_fusion.2
  151.5 11.6 %fusion.134 = (f32[1024]{0:T(1024)}, f32[1024,1024]{1,0:T(8,128)}, bf16[1024,1024]{1,0:T(8,128)(2,1)}) fusion(f32[1,1024,1024]{2,1,0:T(8,128)} %get-tuple-element.807, f32[1024,1024]{1,0:T(8,128)} %get-tuple-element.849, f32[1024]{0:T(1024)S(1)} %broadcast_multiply_fusion.8, f32[1024,1024]{1,0:T(8,128)} %get-tuple-element.803, ...), kind=kLoop, calls=%fused_computation.189 | loop fusion | flops 27261952 | bytes 27283456 | tf_op jit(solution)/shard_map/transpose(jvp())/reduce_sum | solution.py:83
  163.0 7.2 reshape.973
  170.3 7.7 copy.225
  182.8 203.6 %while.43 = (s32[]{:T(128)}, f32[16]{0:T(128)}, f32[1,16,64,128]{3,2,1,0:T(8,128)}, f32[4,1,256,16,64]{2,4,3,1,0:T(8,128)}, f32[4,1,256,16]{2,0,3,1:T(4,128)}, /...) while((s32[]{:T(128)}, f32[16]{0:T(128)}, ...), condition=%wide.region_23.24_spmd.clone, body=%wide.region_10.23_spmd.clone.sunk | while | flops 3951050752 | bytes 36329996 | solution.py:50
  191.8 2.9 convolution_bitcast_fusion.10
  195.1 8.8 %fusion.257 = (f32[256,16]{0,1:T(8,128)}, f32[256,16]{0,1:T(8,128)}, f32[256,16]{0,1:T(8,128)}, f32[256,256]{1,0:T(8,128)S(1)}) fusion(f32[256,16]{0,1:T(8,128)S(1)} %fusion.255, f32[256,16]{0,1:T(8,128)S(1)} %bitcast.562, f32[256,256]{1,0:T(8,128)S(1)} %fusion.256, pred[256,256]{1,0:T(8,128)(4,1)S(1)} %bitcast.570, ...), kind=kOutput, calls=%fused_computation.73.clone.1 | convolution fusion | flops 820957184 | bytes 2768896 | tf_op jit(solution)/shard_map/transpose(jvp(vmap()))/while/body/eval_jaxpr/checkpoint/ijh,jhp->ihp/dot_general | solution.py:40
  209.0 3.4 fusion.258
  217.7 6.0 fusion.263
  242.9 2.9 convolution_bitcast_fusion.10
  246.2 8.8 %fusion.257 = (f32[256,16]{0,1:T(8,128)}, f32[256,16]{0,1:T(8,128)}, f32[256,16]{0,1:T(8,128)}, f32[256,256]{1,0:T(8,128)S(1)}) fusion(f32[256,16]{0,1:T(8,128)S(1)} %fusion.255, f32[256,16]{0,1:T(8,128)S(1)} %bitcast.562, f32[256,256]{1,0:T(8,128)S(1)} %fusion.256, pred[256,256]{1,0:T(8,128)(4,1)S(1)} %bitcast.570, ...), kind=kOutput, calls=%fused_computation.73.clone.1 | convolution fusion | flops 820957184 | bytes 2768896 | tf_op jit(solution)/shard_map/transpose(jvp(vmap()))/while/body/eval_jaxpr/checkpoint/ijh,jhp->ihp/dot_general | solution.py:40
  260.0 3.4 fusion.258
  268.7 6.0 fusion.263
  297.2 8.8 %fusion.257 = (f32[256,16]{0,1:T(8,128)}, f32[256,16]{0,1:T(8,128)}, f32[256,16]{0,1:T(8,128)}, f32[256,256]{1,0:T(8,128)S(1)}) fusion(f32[256,16]{0,1:T(8,128)S(1)} %fusion.255, f32[256,16]{0,1:T(8,128)S(1)} %bitcast.562, f32[256,256]{1,0:T(8,128)S(1)} %fusion.256, pred[256,256]{1,0:T(8,128)(4,1)S(1)} %bitcast.570, ...), kind=kOutput, calls=%fused_computation.73.clone.1 | convolution fusion | flops 820957184 | bytes 2768896 | tf_op jit(solution)/shard_map/transpose(jvp(vmap()))/while/body/eval_jaxpr/checkpoint/ijh,jhp->ihp/dot_general | solution.py:40
  311.0 3.4 fusion.258
  319.7 6.0 fusion.263
  348.2 8.8 %fusion.257 = (f32[256,16]{0,1:T(8,128)}, f32[256,16]{0,1:T(8,128)}, f32[256,16]{0,1:T(8,128)}, f32[256,256]{1,0:T(8,128)S(1)}) fusion(f32[256,16]{0,1:T(8,128)S(1)} %fusion.255, f32[256,16]{0,1:T(8,128)S(1)} %bitcast.562, f32[256,256]{1,0:T(8,128)S(1)} %fusion.256, pred[256,256]{1,0:T(8,128)(4,1)S(1)} %bitcast.570, ...), kind=kOutput, calls=%fused_computation.73.clone.1 | convolution fusion | flops 820957184 | bytes 2768896 | tf_op jit(solution)/shard_map/transpose(jvp(vmap()))/while/body/eval_jaxpr/checkpoint/ijh,jhp->ihp/dot_general | solution.py:40
  362.1 3.4 fusion.258
  370.7 6.0 fusion.263
  386.4 8.1 copy.238
  394.5 7.6 reshape.974
  402.2 11.9 %multiply_reduce_fusion.5 = (f32[1024]{0:T(1024)S(1)}, f32[1024]{0:T(1024)S(1)}, f32[1024]{0:T(1024)S(1)}, bf16[1024]{0:T(1024)(128)(2,1)S(1)}, f32[1024]{0:T(1024)S(1)}, /*index=5*/f32[1,1024,1024]{2,1,0:T(8,128)S(1)}) fusion(f32[1,1024,1024]{2,1,0:T(8,128)} %bitcast.559, f32[1024,1024]{1,0:T(8,128)} %copy-done.4, f32[1,1024,1024]{2,1,0:T(8,128)} %get-tuple-element.807, ...), kind=kLoop, calls=%fused_computation.194 | loop fusion | flops 20966400 | bytes 25188352 | tf_op jit(solution)/shard_map/transpose(jvp())/reduce_sum | solution.py:22
  414.1 5.4 broadcast_multiply_fusion
  419.5 7.0 fusion.137
  436.9 6.1 convolution_convert_fusion.1
  443.1 3.8 convolution_convert_fusion.2
  446.8 4.0 convolution_convert_fusion
  450.9 3.3 fusion.166
  456.6 82.2 %all-reduce.23 = (bf16[1024,16]{0,1:T(8,128)(2,1)S(1)}, bf16[4,1024]{1,0:T(4,128)(2,1)S(1)}, bf16[1024]{0:T(1024)(128)(2,1)S(1)}, bf16[16]{0:T(256)(128)(2,1)S(1...) all-reduce(bf16[1024,16]{0,1:T(8,128)(2,1)S(1)} %convolution_conver, ...), channel_id=1, replica_groups=mesh['dp'=16,'tensor'=2] {'dp'}, use_global_device_ids=true, to_apply=%region_30.31 | all-reduce | flops 22576 | bytes 90304 | tf_op jit(solution)/shard_map/psum | solution.py:209
  547.7 37.6 %all-reduce.22 = (f32[1024]{0:T(1024)}, f32[4,256]{1,0:T(4,128)}, f32[256]{0:T(256)}) all-reduce(f32[1024]{0:T(1024)S(1)} %multiply_reduce_fusion.10, f32[4,256]{1,0:T(4,128)S(1)} %pad_add_fusion.6, f32[256]{0:T(256)S(1)} %get-tuple-element.727), channel_id=1, replica_groups=mesh['dp'=16,'tensor'=2] {'dp','tensor'}, use_global_device_ids=true, to_apply=%region_27.28 | all-reduce | flops 2304 | bytes 18432 | tf_op jit(solution)/shard_map/psum | solution.py:218
  585.3 5.6 add_convert_fusion
  591.0 100.4 %all-reduce.32.cloned.1.call-done = (bf16[1024,1024]{1,0:T(8,128)(2,1)}, bf16[1024,1024]{1,0:T(8,128)(2,1)}, bf16[1024,1024]{1,0:T(8,128)(2,1)}) async-done(((bf16[1024,1024]{1,0:T(8,128)(2,1)}, bf16[1024,1024]{1,0:T(8,128)(2,1)}, bf16[1024,1024]{1,0:T(8,128)(2,1)}), (bf16[1024,1024]{1,0:T(8,128)(2,1)}, bf16[1024,1024]{1,0:T(8,128)(2,1)}, bf16[1024,1024]{1,0:T(8,128)(2,1)})) %all-reduce.32.cloned.1.call-update) | async-done | bytes 6291472 | tf_op jit(solution)/shard_map/psum | solution.py:207
  691.4 4.2 convert_element_type.123
  700.5 126.2 %all-reduce.30.cloned.1.call-done = f32[1024,256]{1,0:T(8,128)} async-done(((f32[1024,256]{1,0:T(8,128)}), f32[1024,256]{1,0:T(8,128)}) %all-reduce.30.cloned.1.call-update) | async-done | bytes 1048592 | tf_op jit(solution)/shard_map/psum | solution.py:218
  (647 shorter events, 207.6 us)
Async XLA Ops:
  7.2 118.3 %copy-start = (bf16[1024,1024]{1,0:T(8,128)(2,1)S(1)}, bf16[1024,1024]{1,0:T(8,128)(2,1)}, u32[]{:S(2)}) copy-start(bf16[1024,1024]{1,0:T(8,128)(2,1)} %param.22) | copy-start | bytes 6291460
  7.2 535.6 %all-reduce.34.cloned.1.call-start = ((), (), s32[]{:S(2)}) async-start(), calls=%async_computation.2 | async-start | bytes 8388608 | tf_op jit(solution)/shard_map/psum | solution.py:150
  34.5 10.7 %copy-start.87 = (f32[16]{0:T(128)S(1)}, f32[16]{0:T(128)}, u32[]{:S(2)}) copy-start(f32[16]{0:T(128)} %param.31) | copy-start | bytes 196
  125.5 26.0 %copy-start.52 = (f32[1024]{0:T(1024)}, f32[1024]{0:T(1024)S(1)}, u32[]{:S(2)}) copy-start(f32[1024]{0:T(1024)S(1)} %mul.773) | copy-start | bytes 12292
  125.5 11.6 %copy-start.77 = (f32[1024]{0:T(1024)S(1)}, f32[1024]{0:T(1024)}, u32[]{:S(2)}) copy-start(f32[1024]{0:T(1024)} %param.33) | copy-start | bytes 12292
  137.1 14.3 %copy-start.63 = (f32[1024]{0:T(1024)}, f32[1024]{0:T(1024)S(1)}, u32[]{:S(2)}) copy-start(f32[1024]{0:T(1024)S(1)} %add_rsqrt_fusion) | copy-start | bytes 12292
  189.5 14.5 %copy-start.31 = (pred[256,256,1]{1,0,2:T(8,128)(4,1)}, pred[256,256,1]{1,0,2:T(8,128)(4,1)S(1)}, u32[]{:S(2)}) copy-start(pred[256,256,1]{1,0,2:T(8,128)(4,1)S(1)} %iota_compare_fusion.3) | copy-start | bytes 196612 | tf_op jit(solution)/shard_map/transpose(jvp(vmap()))/while
  191.8 12.1 %copy-start.19 = (f32[256,16]{0,1:T(8,128)}, f32[256,16]{0,1:T(8,128)S(1)}, u32[]{:S(2)}) copy-start(f32[256,16]{0,1:T(8,128)S(1)} %get-tuple-element.1042) | copy-start | bytes 49156 | tf_op jit(solution)/shard_map/transpose(jvp(vmap()))/while
  195.1 10.3 %copy-start.1 = (f32[1,16,64,128]{3,2,1,0:T(8,128)S(1)}, f32[1,16,64,128]{3,2,1,0:T(8,128)}, u32[]{:S(2)}) copy-start(f32[1,16,64,128]{3,2,1,0:T(8,128)} %broadcast_select_fusion.3) | copy-start | bytes 1572868 | tf_op jit(solution)/shard_map/transpose(jvp(vmap()))/while
  195.1 10.3 %copy-start.3 = (f32[1,16,64,128]{3,2,1,0:T(8,128)S(1)}, f32[1,16,64,128]{3,2,1,0:T(8,128)}, u32[]{:S(2)}) copy-start(f32[1,16,64,128]{3,2,1,0:T(8,128)} %dynamic-slice_bitcast_fusion.10) | copy-start | bytes 1572868 | tf_op jit(solution)/shard_map/transpose(jvp(vmap()))/while
  217.6 10.1 %copy-start.12 = (f32[1,256,16]{1,2,0:T(8,128)S(1)}, f32[1,256,16]{1,2,0:T(8,128)}, u32[]{:S(2)}) copy-start(f32[1,256,16]{1,2,0:T(8,128)} %get-tuple-element.1034) | copy-start | bytes 49156 | tf_op jit(solution)/shard_map/transpose(jvp(vmap()))/while
  217.6 10.1 %copy-start.14 = (f32[256,16]{0,1:T(8,128)S(1)}, f32[256,16]{0,1:T(8,128)}, u32[]{:S(2)}) copy-start(f32[256,16]{0,1:T(8,128)} %copy-done.13) | copy-start | bytes 49156 | tf_op jit(solution)/shard_map/transpose(jvp(vmap()))/while
  217.6 10.1 %copy-start.34 = (f32[1,1,16]{1,2,0:T(8,128)S(1)}, f32[1,1,16]{1,2,0:T(8,128)}, u32[]{:S(2)}) copy-start(f32[1,1,16]{1,2,0:T(8,128)} %get-tuple-element.1040) | copy-start | bytes 196 | tf_op jit(solution)/shard_map/transpose(jvp(vmap()))/while
  217.6 10.1 %copy-start.39 = (f32[256,16]{0,1:T(8,128)S(1)}, f32[256,16]{0,1:T(8,128)}, u32[]{:S(2)}) copy-start(f32[256,16]{0,1:T(8,128)} %get-tuple-element.1038) | copy-start | bytes 49156 | tf_op jit(solution)/shard_map/transpose(jvp(vmap()))/while
  240.5 14.5 %copy-start.31 = (pred[256,256,1]{1,0,2:T(8,128)(4,1)}, pred[256,256,1]{1,0,2:T(8,128)(4,1)S(1)}, u32[]{:S(2)}) copy-start(pred[256,256,1]{1,0,2:T(8,128)(4,1)S(1)} %iota_compare_fusion.3) | copy-start | bytes 196612 | tf_op jit(solution)/shard_map/transpose(jvp(vmap()))/while
  242.9 12.1 %copy-start.19 = (f32[256,16]{0,1:T(8,128)}, f32[256,16]{0,1:T(8,128)S(1)}, u32[]{:S(2)}) copy-start(f32[256,16]{0,1:T(8,128)S(1)} %get-tuple-element.1042) | copy-start | bytes 49156 | tf_op jit(solution)/shard_map/transpose(jvp(vmap()))/while
  246.1 10.3 %copy-start.1 = (f32[1,16,64,128]{3,2,1,0:T(8,128)S(1)}, f32[1,16,64,128]{3,2,1,0:T(8,128)}, u32[]{:S(2)}) copy-start(f32[1,16,64,128]{3,2,1,0:T(8,128)} %broadcast_select_fusion.3) | copy-start | bytes 1572868 | tf_op jit(solution)/shard_map/transpose(jvp(vmap()))/while
  246.1 10.3 %copy-start.3 = (f32[1,16,64,128]{3,2,1,0:T(8,128)S(1)}, f32[1,16,64,128]{3,2,1,0:T(8,128)}, u32[]{:S(2)}) copy-start(f32[1,16,64,128]{3,2,1,0:T(8,128)} %dynamic-slice_bitcast_fusion.10) | copy-start | bytes 1572868 | tf_op jit(solution)/shard_map/transpose(jvp(vmap()))/while
  268.6 10.1 %copy-start.12 = (f32[1,256,16]{1,2,0:T(8,128)S(1)}, f32[1,256,16]{1,2,0:T(8,128)}, u32[]{:S(2)}) copy-start(f32[1,256,16]{1,2,0:T(8,128)} %get-tuple-element.1034) | copy-start | bytes 49156 | tf_op jit(solution)/shard_map/transpose(jvp(vmap()))/while
  268.6 10.1 %copy-start.14 = (f32[256,16]{0,1:T(8,128)S(1)}, f32[256,16]{0,1:T(8,128)}, u32[]{:S(2)}) copy-start(f32[256,16]{0,1:T(8,128)} %copy-done.13) | copy-start | bytes 49156 | tf_op jit(solution)/shard_map/transpose(jvp(vmap()))/while
  268.7 10.1 %copy-start.34 = (f32[1,1,16]{1,2,0:T(8,128)S(1)}, f32[1,1,16]{1,2,0:T(8,128)}, u32[]{:S(2)}) copy-start(f32[1,1,16]{1,2,0:T(8,128)} %get-tuple-element.1040) | copy-start | bytes 196 | tf_op jit(solution)/shard_map/transpose(jvp(vmap()))/while
  268.7 10.1 %copy-start.39 = (f32[256,16]{0,1:T(8,128)S(1)}, f32[256,16]{0,1:T(8,128)}, u32[]{:S(2)}) copy-start(f32[256,16]{0,1:T(8,128)} %get-tuple-element.1038) | copy-start | bytes 49156 | tf_op jit(solution)/shard_map/transpose(jvp(vmap()))/while
  291.5 14.5 %copy-start.31 = (pred[256,256,1]{1,0,2:T(8,128)(4,1)}, pred[256,256,1]{1,0,2:T(8,128)(4,1)S(1)}, u32[]{:S(2)}) copy-start(pred[256,256,1]{1,0,2:T(8,128)(4,1)S(1)} %iota_compare_fusion.3) | copy-start | bytes 196612 | tf_op jit(solution)/shard_map/transpose(jvp(vmap()))/while
  293.9 12.1 %copy-start.19 = (f32[256,16]{0,1:T(8,128)}, f32[256,16]{0,1:T(8,128)S(1)}, u32[]{:S(2)}) copy-start(f32[256,16]{0,1:T(8,128)S(1)} %get-tuple-element.1042) | copy-start | bytes 49156 | tf_op jit(solution)/shard_map/transpose(jvp(vmap()))/while
  297.2 10.3 %copy-start.1 = (f32[1,16,64,128]{3,2,1,0:T(8,128)S(1)}, f32[1,16,64,128]{3,2,1,0:T(8,128)}, u32[]{:S(2)}) copy-start(f32[1,16,64,128]{3,2,1,0:T(8,128)} %broadcast_select_fusion.3) | copy-start | bytes 1572868 | tf_op jit(solution)/shard_map/transpose(jvp(vmap()))/while
  297.2 10.3 %copy-start.3 = (f32[1,16,64,128]{3,2,1,0:T(8,128)S(1)}, f32[1,16,64,128]{3,2,1,0:T(8,128)}, u32[]{:S(2)}) copy-start(f32[1,16,64,128]{3,2,1,0:T(8,128)} %dynamic-slice_bitcast_fusion.10) | copy-start | bytes 1572868 | tf_op jit(solution)/shard_map/transpose(jvp(vmap()))/while
  319.7 10.1 %copy-start.12 = (f32[1,256,16]{1,2,0:T(8,128)S(1)}, f32[1,256,16]{1,2,0:T(8,128)}, u32[]{:S(2)}) copy-start(f32[1,256,16]{1,2,0:T(8,128)} %get-tuple-element.1034) | copy-start | bytes 49156 | tf_op jit(solution)/shard_map/transpose(jvp(vmap()))/while
  319.7 10.1 %copy-start.14 = (f32[256,16]{0,1:T(8,128)S(1)}, f32[256,16]{0,1:T(8,128)}, u32[]{:S(2)}) copy-start(f32[256,16]{0,1:T(8,128)} %copy-done.13) | copy-start | bytes 49156 | tf_op jit(solution)/shard_map/transpose(jvp(vmap()))/while
  319.7 10.1 %copy-start.34 = (f32[1,1,16]{1,2,0:T(8,128)S(1)}, f32[1,1,16]{1,2,0:T(8,128)}, u32[]{:S(2)}) copy-start(f32[1,1,16]{1,2,0:T(8,128)} %get-tuple-element.1040) | copy-start | bytes 196 | tf_op jit(solution)/shard_map/transpose(jvp(vmap()))/while
  319.7 10.1 %copy-start.39 = (f32[256,16]{0,1:T(8,128)S(1)}, f32[256,16]{0,1:T(8,128)}, u32[]{:S(2)}) copy-start(f32[256,16]{0,1:T(8,128)} %get-tuple-element.1038) | copy-start | bytes 49156 | tf_op jit(solution)/shard_map/transpose(jvp(vmap()))/while
  342.6 14.5 %copy-start.31 = (pred[256,256,1]{1,0,2:T(8,128)(4,1)}, pred[256,256,1]{1,0,2:T(8,128)(4,1)S(1)}, u32[]{:S(2)}) copy-start(pred[256,256,1]{1,0,2:T(8,128)(4,1)S(1)} %iota_compare_fusion.3) | copy-start | bytes 196612 | tf_op jit(solution)/shard_map/transpose(jvp(vmap()))/while
  344.9 12.1 %copy-start.19 = (f32[256,16]{0,1:T(8,128)}, f32[256,16]{0,1:T(8,128)S(1)}, u32[]{:S(2)}) copy-start(f32[256,16]{0,1:T(8,128)S(1)} %get-tuple-element.1042) | copy-start | bytes 49156 | tf_op jit(solution)/shard_map/transpose(jvp(vmap()))/while
  348.2 10.3 %copy-start.1 = (f32[1,16,64,128]{3,2,1,0:T(8,128)S(1)}, f32[1,16,64,128]{3,2,1,0:T(8,128)}, u32[]{:S(2)}) copy-start(f32[1,16,64,128]{3,2,1,0:T(8,128)} %broadcast_select_fusion.3) | copy-start | bytes 1572868 | tf_op jit(solution)/shard_map/transpose(jvp(vmap()))/while
  348.2 10.3 %copy-start.3 = (f32[1,16,64,128]{3,2,1,0:T(8,128)S(1)}, f32[1,16,64,128]{3,2,1,0:T(8,128)}, u32[]{:S(2)}) copy-start(f32[1,16,64,128]{3,2,1,0:T(8,128)} %dynamic-slice_bitcast_fusion.10) | copy-start | bytes 1572868 | tf_op jit(solution)/shard_map/transpose(jvp(vmap()))/while
  370.7 10.1 %copy-start.12 = (f32[1,256,16]{1,2,0:T(8,128)S(1)}, f32[1,256,16]{1,2,0:T(8,128)}, u32[]{:S(2)}) copy-start(f32[1,256,16]{1,2,0:T(8,128)} %get-tuple-element.1034) | copy-start | bytes 49156 | tf_op jit(solution)/shard_map/transpose(jvp(vmap()))/while
  370.7 10.1 %copy-start.14 = (f32[256,16]{0,1:T(8,128)S(1)}, f32[256,16]{0,1:T(8,128)}, u32[]{:S(2)}) copy-start(f32[256,16]{0,1:T(8,128)} %copy-done.13) | copy-start | bytes 49156 | tf_op jit(solution)/shard_map/transpose(jvp(vmap()))/while
  370.7 10.1 %copy-start.34 = (f32[1,1,16]{1,2,0:T(8,128)S(1)}, f32[1,1,16]{1,2,0:T(8,128)}, u32[]{:S(2)}) copy-start(f32[1,1,16]{1,2,0:T(8,128)} %get-tuple-element.1040) | copy-start | bytes 196 | tf_op jit(solution)/shard_map/transpose(jvp(vmap()))/while
  370.7 10.1 %copy-start.39 = (f32[256,16]{0,1:T(8,128)S(1)}, f32[256,16]{0,1:T(8,128)}, u32[]{:S(2)}) copy-start(f32[256,16]{0,1:T(8,128)} %get-tuple-element.1038) | copy-start | bytes 49156 | tf_op jit(solution)/shard_map/transpose(jvp(vmap()))/while
  370.7 10.1 %copy-start.40 = (f32[256,16]{0,1:T(8,128)S(1)}, f32[256,16]{0,1:T(8,128)}, u32[]{:S(2)}) copy-start(f32[256,16]{0,1:T(8,128)} %get-tuple-element.1037) | copy-start | bytes 49156 | tf_op jit(solution)/shard_map/transpose(jvp(vmap()))/while
  402.1 11.9 %copy-start.42 = (f32[4,1,256,16]{2,0,3,1:T(4,128)S(1)}, f32[4,1,256,16]{2,0,3,1:T(4,128)}, u32[]{:S(2)}) copy-start(f32[4,1,256,16]{2,0,3,1:T(4,128)} %get-tuple-element.449) | copy-start | bytes 196612
  402.1 12.0 %copy-start.55 = (f32[1,1024]{1,0:T(1,128)S(1)}, f32[1,1024]{1,0:T(1,128)}, u32[]{:S(2)}) copy-start(f32[1,1024]{1,0:T(1,128)} %copy-done.54) | copy-start | bytes 12292
  402.1 12.0 %copy-start.57 = (f32[1,1024]{1,0:T(1,128)S(1)}, f32[1,1024]{1,0:T(1,128)}, u32[]{:S(2)}) copy-start(f32[1,1024]{1,0:T(1,128)} %copy-done.56) | copy-start | bytes 12292
  402.1 12.0 %copy-start.59 = (f32[1,1024]{1,0:T(1,128)S(1)}, f32[1,1024]{1,0:T(1,128)}, u32[]{:S(2)}) copy-start(f32[1,1024]{1,0:T(1,128)} %copy-done.58) | copy-start | bytes 12292
  402.2 12.0 %copy-start.61 = (f32[1,1024]{1,0:T(1,128)S(1)}, f32[1,1024]{1,0:T(1,128)}, u32[]{:S(2)}) copy-start(f32[1,1024]{1,0:T(1,128)} %copy-done.60) | copy-start | bytes 12292
  436.7 254.7 %all-reduce.32.cloned.1.call-start = ((), (), s32[]{:S(2)}) async-start(), calls=%async_computation.1 | async-start | bytes 12582912 | tf_op jit(solution)/shard_map/psum | solution.py:207
  450.9 375.9 %all-reduce.30.cloned.1.call-start = ((), (), s32[]{:S(2)}) async-start(), calls=%async_computation | async-start | bytes 2097152 | tf_op jit(solution)/shard_map/psum | solution.py:218
  454.3 91.3 %copy-start.48 = (f32[1024]{0:T(1024)S(1)}, f32[1024]{0:T(1024)}, u32[]{:S(2)}) copy-start(f32[1024]{0:T(1024)} %copy-done.47) | copy-start | bytes 12292
  454.3 91.3 %copy-start.51 = (f32[1024]{0:T(1024)S(1)}, f32[1024]{0:T(1024)}, u32[]{:S(2)}) copy-start(f32[1024]{0:T(1024)} %param.21) | copy-start | bytes 12292
  (116 other events, 620.4 us)
Sparse Core Ops, SparseCore 0:
  436.8 31.0 all-reduce.33
  476.6 214.6 all-reduce.31
  698.0 128.7 all-reduce.29
where the time goes:
time: 843 us; the launch traced here: 836 us
  waiting for transfers between devices  227 us (27%)
  matrix products  221 us (26%)
  local copies, waits for them, and re-layouts  125 us (15%)
  blocking collectives  125 us (15%)
  other arithmetic  121 us (14%)
  between operations  14.8 us (2%)
    psum x1, waiting for transfers between devices, per_device(): lax.psum((bc_proj_grad, bc_conv_grad, bc_conv_bias_grad, norm_gain_grad),...  126 us
    psum x1, waiting for transfers between devices, per_device(): lax.psum(z_proj_grad.astype(jnp.bfloat16), 'dp').astype(jnp.float32)  100 us
    dot_general x12, matrix products, advance(): within = jnp.einsum('ijh,jhp->ihp', mixing, block_vals, precision=HIGH)  87.9 us
    psum x1, blocking collectives, per_device(): lax.psum(dt_proj_grad.astype(jnp.bfloat16), 'dp').astype(jnp.float32)  82.2 us
    psum x1, blocking collectives, per_device(): lax.psum((bc_proj_grad, bc_conv_grad, bc_conv_bias_grad, norm_gain_grad),...  37.6 us
    dot_general x16, matrix products, advance(): jnp.einsum('in,hpn->ihp', block_c, inner_state, precision=HIGH)  34.4 us
    dot_general x12, matrix products, advance(): jnp.einsum('jh,jn,jhp->hpn', tail_gain, block_b, block_vals, precision=HIGH)  32.9 us
    another operation x36, other arithmetic  24.2 us
  transfers between devices with their start and end apart: 3, of which 2 were waited for; matrix products, arithmetic and copies ran while one was open for 5% of the time, Pallas kernels for 0%

commit v1 on v0

v1 whole, which is shorter than its diff:
```python
import jax
import jax.numpy as jnp
from jax import lax
from jax.experimental import pallas as pl
from jax.experimental.pallas import tpu as pltpu
from jax.sharding import PartitionSpec as P

INNER = 2048
STRETCH = 256
SEQ_LEN = 1024
EPS = 1e-05
HIGH = lax.Precision.HIGHEST
CHUNKS = SEQ_LEN // STRETCH
LANES = 128
F32 = jnp.float32
BF16 = jnp.bfloat16


def causal_conv(sequence, weights, offsets):
    row_count, channels = sequence.shape
    kernel_width = weights.shape[0]
    blocked = sequence.reshape(row_count // SEQ_LEN, SEQ_LEN, channels)
    padded = jnp.pad(blocked, ((0, 0), (kernel_width - 1, 0), (0, 0)))
    summed = jnp.zeros_like(blocked) + offsets
    for offset in range(kernel_width):
        summed = summed + weights[offset] * padded[:, offset : offset + SEQ_LEN]
    return jax.nn.silu(summed).reshape(row_count, channels)


def nn(left, right):
    return jnp.dot(left, right, preferred_element_type=F32)


def nt(left, right):
    return lax.dot_general(left, right, (((1,), (1,)), ((), ())), preferred_element_type=F32)


def tn(left, right):
    return lax.dot_general(left, right, (((0,), (0,)), ((), ())), preferred_element_type=F32)


def first_half(shape):
    return lax.broadcasted_iota(jnp.int32, shape, 1) < LANES // 2


def spread(pair):
    rows = pair.shape[0]
    return jnp.where(
        first_half((rows, LANES)),
        jnp.broadcast_to(pair[:, 0:1], (rows, LANES)),
        jnp.broadcast_to(pair[:, 1:2], (rows, LANES)),
    )


def head_sums(wide):
    first = first_half(wide.shape)
    return jnp.concatenate(
        [
            jnp.sum(jnp.where(first, wide, 0.0), axis=1, keepdims=True),
            jnp.sum(jnp.where(first, 0.0, wide), axis=1, keepdims=True),
        ],
        axis=1,
    )


def shifted_rows(x_ref, chunk):
    start = chunk * STRETCH
    if chunk == 0:
        extended = jnp.concatenate([jnp.zeros((8, LANES), F32), x_ref[0:STRETCH, :]], axis=0)
    else:
        extended = x_ref[start - 8 : start + STRETCH, :]
    return [extended[8:]] + [pltpu.roll(extended, s, 0)[8:] for s in (1, 2, 3)]


def convolved(shifted, w_ref, bias_ref):
    total = bias_ref[...] + w_ref[3:4, :] * shifted[0]
    for s in (1, 2, 3):
        total = total + w_ref[3 - s : 4 - s, :] * shifted[s]
    return total


def forward_kernel(
    x_ref, z_ref, gi_ref, b_ref, c_ref, bt_ref, dt_ref, cum_ref, row_ref,
    w_ref, bias_ref, skip_ref, gain_ref,
    scan_ref, state_ref, stat_ref,
    scores, squares, inners,
):
    group = pl.program_id(0)
    groups = pl.num_programs(0)

    @pl.when(group == 0)
    def _():
        squares[...] = jnp.zeros_like(squares)
        inners[...] = jnp.zeros_like(inners)
        for chunk in range(CHUNKS):
            rows = slice(chunk * STRETCH, (chunk + 1) * STRETCH)
            scores[chunk] = nt(c_ref[rows, :], b_ref[rows, :])

    lower = lax.broadcasted_iota(jnp.int32, (STRETCH, STRETCH), 0) >= lax.broadcasted_iota(
        jnp.int32, (STRETCH, STRETCH), 1
    )
    first = first_half((STRETCH, LANES))
    state = jnp.zeros((b_ref.shape[1], LANES), F32)
    for chunk in range(CHUNKS):
        rows = slice(chunk * STRETCH, (chunk + 1) * STRETCH)
        state_ref[0, chunk] = state
        conv = convolved(shifted_rows(x_ref, chunk), w_ref, bias_ref)
        mixed = conv * jax.nn.sigmoid(conv)
        cum = cum_ref[0, rows, :]
        cum_wide = spread(cum)
        last = cum_wide[STRETCH - 1 : STRETCH, :]
        dtx = mixed * spread(dt_ref[0, rows, :])
        dtx_low = dtx.astype(BF16)
        within = []
        for head in range(2):
            gap = cum[:, head : head + 1] - row_ref[0, head : head + 1, rows]
            decay = jnp.exp(jnp.where(lower, gap, -1e30))
            within.append(nn((scores[chunk] * decay).astype(BF16), dtx_low))
        carried = jnp.exp(cum_wide) * nn(c_ref[rows, :], state.astype(BF16))
        scanned = jnp.where(first, within[0], within[1]) + carried + skip_ref[...] * mixed
        scan_ref[rows, :] = scanned
        tail = (jnp.exp(last - cum_wide) * dtx).astype(BF16)
        state = jnp.exp(last) * state + nn(bt_ref[:, rows], tail)
        z = z_ref[rows, :]
        gated = scanned * (z * jax.nn.sigmoid(z))
        squares[rows, :] += gated * gated
        inners[rows, :] += gi_ref[rows, :] * gain_ref[...] * gated

    @pl.when(group == groups - 1)
    def _():
        stat_ref[...] = jnp.concatenate(
            [
                jnp.sum(squares[...], axis=1, keepdims=True),
                jnp.sum(inners[...], axis=1, keepdims=True),
            ],
            axis=1,
        )


def backward_kernel(
    x_ref, z_ref, gi_ref, scan_ref, stat_ref, b_ref, c_ref, ct_ref, dt_ref, cum_ref, row_ref,
    state_ref, w_ref, bias_ref, skip_ref, gain_ref,
    x_low_ref, ddt_ref, dcum_ref, param_ref, db_ref, dc_ref,
    scores, score_grad,
):
    group = pl.program_id(0)
    groups = pl.num_programs(0)

    @pl.when(group == 0)
    def _():
        score_grad[...] = jnp.zeros_like(score_grad)
        db_ref[...] = jnp.zeros_like(db_ref)
        dc_ref[...] = jnp.zeros_like(dc_ref)
        for chunk in range(CHUNKS):
            rows = slice(chunk * STRETCH, (chunk + 1) * STRETCH)
            scores[chunk] = nt(b_ref[rows, :], c_ref[rows, :])

    upper = lax.broadcasted_iota(jnp.int32, (STRETCH, STRETCH), 0) <= lax.broadcasted_iota(
        jnp.int32, (STRETCH, STRETCH), 1
    )
    first = first_half((STRETCH, LANES))
    at_end = lax.broadcasted_iota(jnp.int32, (STRETCH, LANES), 0) == STRETCH - 1
    state_grad = jnp.zeros((b_ref.shape[1], LANES), F32)
    following = jnp.zeros((8, LANES), F32)
    sums = [jnp.zeros((1, LANES), F32) for _ in range(6)]
    for chunk in reversed(range(CHUNKS)):
        rows = slice(chunk * STRETCH, (chunk + 1) * STRETCH)
        rms = stat_ref[rows, 0:1]
        inner = stat_ref[rows, 1:2]
        z = z_ref[rows, :]
        scanned = scan_ref[rows, :]
        gate = z * jax.nn.sigmoid(z)
        hat = scanned * gate * rms
        dy = rms * (gi_ref[rows, :] * gain_ref[...] - hat * inner) * gate

        shifted = shifted_rows(x_ref, chunk)
        conv = convolved(shifted, w_ref, bias_ref)
        sig = jax.nn.sigmoid(conv)
        mixed = conv * sig
        cum = cum_ref[0, rows, :]
        cum_wide = spread(cum)
        last = cum_wide[STRETCH - 1 : STRETCH, :]
        dt_wide = spread(dt_ref[0, rows, :])
        dtx = mixed * dt_wide
        dtx_low = dtx.astype(BF16)
        dy_low = dy.astype(BF16)
        dtx_back = []
        pair_grad = None
        for head in range(2):
            gap = row_ref[0, head : head + 1, rows] - cum[:, head : head + 1]
            decay = jnp.exp(jnp.where(upper, gap, -1e30))
            dtx_back.append(nn((scores[chunk] * decay).astype(BF16), dy_low))
            own = jnp.where(first if head == 0 else ~first, dy, 0.0).astype(BF16)
            term = nt(dtx_low, own) * decay
            pair_grad = term if pair_grad is None else pair_grad + term
        score_grad[chunk] += pair_grad
        state = state_ref[0, chunk]
        grow = jnp.exp(cum_wide)
        fall = jnp.exp(last - cum_wide)
        state_grad_low = state_grad.astype(BF16)
        arrival = fall * nn(b_ref[rows, :], state_grad_low)
        dtx_grad = jnp.where(first, dtx_back[0], dtx_back[1]) + arrival
        extra = jnp.sum(dtx_low.astype(F32) * arrival, axis=0, keepdims=True) + jnp.exp(last) * jnp.sum(
            state * state_grad, axis=0, keepdims=True
        )
        dy_grown = (grow * dy).astype(BF16)
        db_ref[rows, :] += nt((fall * dtx).astype(BF16), state_grad_low)
        dc_ref[rows, :] += nt(dy_grown, state.astype(BF16))
        state_grad = jnp.exp(last) * state_grad + nn(ct_ref[:, rows], dy_grown)

        balance = dy_low.astype(F32) * (scanned - skip_ref[...] * mixed) - (
            dtx_low.astype(F32) * dtx_grad
        )
        dcum_ref[0, rows, :] = head_sums(balance + jnp.where(at_end, extra, 0.0))
        ddt_ref[0, rows, :] = head_sums(mixed * dtx_grad)
        conv_grad = (dt_wide * dtx_grad + skip_ref[...] * dy) * (sig * (1.0 + conv * (1.0 - sig)))
        extended = jnp.concatenate([conv_grad, following], axis=0)
        following = conv_grad[0:8]
        back = w_ref[3:4, :] * conv_grad
        for s in (1, 2, 3):
            back = back + w_ref[3 - s : 4 - s, :] * pltpu.roll(extended, STRETCH + 8 - s, 0)[:STRETCH]
        x_low_ref[rows, :] = back.astype(BF16)
        parts = [conv_grad * shifted[3 - k] for k in range(4)] + [conv_grad, dy * mixed]
        sums = [old + jnp.sum(new, axis=0, keepdims=True) for old, new in zip(sums, parts)]
    param_ref[...] = jnp.concatenate(sums + [jnp.zeros((2, LANES), F32)], axis=0)

    @pl.when(group == groups - 1)
    def _():
        for chunk in range(CHUNKS):
            rows = slice(chunk * STRETCH, (chunk + 1) * STRETCH)
            grad = score_grad[chunk].astype(BF16)
            db_ref[rows, :] += nn(grad, c_ref[rows, :])
            dc_ref[rows, :] += tn(grad, b_ref[rows, :])


def wide(rows=SEQ_LEN):
    return pl.BlockSpec((rows, LANES), lambda g: (0, g))


def fixed(*shape):
    return pl.BlockSpec(shape, lambda g: (0,) * len(shape))


def grouped(*shape):
    return pl.BlockSpec((1,) + shape, lambda g: (g,) + (0,) * len(shape))


def by_group(columns):
    rows, heads = columns.shape
    return columns.reshape(rows, heads // 2, 2).transpose(1, 0, 2)


def from_groups(pairs):
    groups, rows, _ = pairs.shape
    return pairs.transpose(1, 0, 2).reshape(rows, groups * 2)


def scan_forward(x_pre, z_pre, gate_in, b_low, c_low, dt3, cum3, row3, x_conv, x_bias, skip, gain):
    channels = x_pre.shape[1]
    groups = channels // LANES
    n = b_low.shape[1]
    return pl.pallas_call(
        forward_kernel,
        grid=(groups,),
        in_specs=[
            wide(), wide(), wide(), fixed(SEQ_LEN, n), fixed(SEQ_LEN, n), fixed(n, SEQ_LEN),
            grouped(SEQ_LEN, 2), grouped(SEQ_LEN, 2), grouped(2, SEQ_LEN),
            wide(4), wide(1), wide(1), wide(1),
        ],
        out_specs=[wide(), grouped(CHUNKS, n, LANES), fixed(SEQ_LEN, 2)],
        out_shape=[
            jax.ShapeDtypeStruct((SEQ_LEN, channels), F32),
            jax.ShapeDtypeStruct((groups, CHUNKS, n, LANES), F32),
            jax.ShapeDtypeStruct((SEQ_LEN, 2), F32),
        ],
        scratch_shapes=[
            pltpu.VMEM((CHUNKS, STRETCH, STRETCH), F32),
            pltpu.VMEM((SEQ_LEN, LANES), F32),
            pltpu.VMEM((SEQ_LEN, LANES), F32),
        ],
        compiler_params=pltpu.CompilerParams(vmem_limit_bytes=32 * 1024 * 1024),
        cost_estimate=pl.CostEstimate(
            flops=2 * 10**9, bytes_accessed=24 * 2**20, transcendentals=groups * 600000
        ),
    )(x_pre, z_pre, gate_in, b_low, c_low, b_low.T, dt3, cum3, row3, x_conv, x_bias, skip, gain)


def scan_backward(
    x_pre, z_pre, gate_in, scanned, stats, b_low, c_low, dt3, cum3, row3, states,
    x_conv, x_bias, skip, gain,
):
    channels = x_pre.shape[1]
    groups = channels // LANES
    n = b_low.shape[1]
    return pl.pallas_call(
        backward_kernel,
        grid=(groups,),
        in_specs=[
            wide(), wide(), wide(), wide(), fixed(SEQ_LEN, 2),
            fixed(SEQ_LEN, n), fixed(SEQ_LEN, n), fixed(n, SEQ_LEN),
            grouped(SEQ_LEN, 2), grouped(SEQ_LEN, 2), grouped(2, SEQ_LEN),
            grouped(CHUNKS, n, LANES), wide(4), wide(1), wide(1), wide(1),
        ],
        out_specs=[
            wide(), grouped(SEQ_LEN, 2), grouped(SEQ_LEN, 2), wide(8),
            fixed(SEQ_LEN, n), fixed(SEQ_LEN, n),
        ],
        out_shape=[
            jax.ShapeDtypeStruct((SEQ_LEN, channels), BF16),
            jax.ShapeDtypeStruct((groups, SEQ_LEN, 2), F32),
            jax.ShapeDtypeStruct((groups, SEQ_LEN, 2), F32),
            jax.ShapeDtypeStruct((8, channels), F32),
            jax.ShapeDtypeStruct((SEQ_LEN, n), F32),
            jax.ShapeDtypeStruct((SEQ_LEN, n), F32),
        ],
        scratch_shapes=[
            pltpu.VMEM((CHUNKS, STRETCH, STRETCH), F32),
            pltpu.VMEM((CHUNKS, STRETCH, STRETCH), F32),
        ],
        compiler_params=pltpu.CompilerParams(vmem_limit_bytes=32 * 1024 * 1024),
        cost_estimate=pl.CostEstimate(
            flops=60 * 10**9, bytes_accessed=200 * 2**20, transcendentals=groups * 800000
        ),
    )(
        x_pre, z_pre, gate_in, scanned, stats, b_low, c_low, c_low.T, dt3, cum3, row3, states,
        x_conv, x_bias, skip, gain,
    )


def over_tensor(value):
    if lax.axis_size("tensor") == 2:
        return value + lax.ppermute(value, "tensor", [(0, 1), (1, 0)])
    return lax.psum(value, "tensor")


def per_device(
    tokens, norm_gain, z_proj, x_proj, dt_proj, bc_proj, x_conv, x_conv_bias, bc_conv,
    bc_conv_bias, dt_bias, a_log, d_skip, gate_gain, out_proj, cotangent,
):
    heads = dt_proj.shape[1]
    channels = x_proj.shape[1]
    head_dim = channels // heads
    width = tokens.shape[1]
    hidden = tokens.astype(F32)
    inv_rms = lax.rsqrt(jnp.mean(hidden * hidden, axis=1, keepdims=True) + EPS)
    normed = hidden * inv_rms
    normed_in = (normed * norm_gain).astype(BF16)
    bc_pre = nn(normed_in, bc_proj)
    dt_pre = nn(normed_in, dt_proj)
    z_pre = nn(normed_in, z_proj)
    x_pre = nn(normed_in, x_proj)
    gate_in_grad = nt(cotangent, out_proj)

    bc_mixed, bc_pull = jax.vjp(causal_conv, bc_pre, bc_conv, bc_conv_bias)
    bc_mixed_low = bc_mixed.astype(BF16)
    state_size = bc_mixed.shape[1] // 2
    b_low, c_low = bc_mixed_low[:, :state_size], bc_mixed_low[:, state_size:]
    step_dt = jax.nn.softplus(dt_pre + dt_bias)
    rate = -jnp.exp(a_log)
    places = jnp.arange(STRETCH)
    lower = (places[:, None] >= places[None, :]).astype(F32)
    cum = jnp.einsum(
        "ij,bjh->bih", lower, (step_dt * rate).reshape(CHUNKS, STRETCH, heads), precision=HIGH
    ).reshape(SEQ_LEN, heads)
    dt3, cum3 = by_group(step_dt), by_group(cum)
    row3 = cum.T.reshape(heads // 2, 2, SEQ_LEN)
    skip = jnp.repeat(d_skip, head_dim)[None, :]
    bias = x_conv_bias[None, :]
    gain = gate_gain[None, :]
    scanned, states, stats = scan_forward(
        x_pre, z_pre, gate_in_grad, b_low, c_low, dt3, cum3, row3, x_conv, bias, skip, gain
    )
    stats = over_tensor(stats)
    gate_rms = lax.rsqrt(stats[:, 0:1] / INNER + EPS)
    inner_mean = stats[:, 1:2] * gate_rms / INNER

    sig_z = jax.nn.sigmoid(z_pre)
    silu_z = z_pre * sig_z
    gate_hat = scanned * silu_z * gate_rms
    gate_out = (gate_hat * gate_gain).astype(BF16)
    gate_gain_grad = jnp.sum(gate_in_grad * gate_hat, axis=0)
    gated_grad = gate_rms * (gate_in_grad * gate_gain - gate_hat * inner_mean)
    z_low = (gated_grad * scanned * (sig_z * (1.0 + z_pre * (1.0 - sig_z)))).astype(BF16)
    out_proj_grad = tn(gate_out, cotangent).astype(BF16)
    z_proj_part = tn(normed_in, z_low)
    out_proj_grad, z_proj_grad = lax.psum((out_proj_grad, z_proj_part.astype(BF16)), "dp")

    x_low, ddt3, dcum3, params, db, dc = scan_backward(
        x_pre, z_pre, gate_in_grad, scanned, jnp.concatenate([gate_rms, inner_mean], axis=1),
        b_low, c_low, dt3, cum3, row3, states, x_conv, bias, skip, gain,
    )
    branch = over_tensor(nn(gate_out, out_proj).astype(BF16)).astype(F32)
    mixed = (hidden + branch).astype(BF16)

    bc_grad, bc_conv_grad, bc_conv_bias_grad = bc_pull(jnp.concatenate([db, dc], axis=1))
    bc_low = bc_grad.astype(BF16)
    decay_grad = jnp.einsum(
        "ji,bjh->bih", lower, from_groups(dcum3).reshape(CHUNKS, STRETCH, heads), precision=HIGH
    ).reshape(SEQ_LEN, heads)
    dt_grad = (decay_grad * rate + from_groups(ddt3)) * jax.nn.sigmoid(dt_pre + dt_bias)
    a_log_grad = jnp.sum(decay_grad * step_dt, axis=0) * rate
    dt_bias_grad = jnp.sum(dt_grad, axis=0)
    dt_low = dt_grad.astype(BF16)
    x_proj_part = tn(normed_in, x_low)
    bc_proj_part = tn(normed_in, bc_low)
    dt_proj_part = tn(normed_in, dt_low)
    norm_part = (
        jnp.sum(z_proj_part * z_proj.astype(F32), axis=1)
        + jnp.sum(x_proj_part * x_proj.astype(F32), axis=1)
        + jnp.sum(bc_proj_part * bc_proj.astype(F32), axis=1)
        + jnp.sum(dt_proj_part * dt_proj.astype(F32), axis=1)
    ) / norm_gain
    bc_proj_part = over_tensor(bc_proj_part.astype(BF16))
    shared = over_tensor(
        jnp.concatenate([norm_part, bc_conv_grad.reshape(-1), bc_conv_bias_grad])
    )
    own = [
        dt_proj_part, params[0:4], params[4], dt_bias_grad, a_log_grad,
        jnp.sum(params[5].reshape(heads, head_dim), axis=1), gate_gain_grad,
    ]
    pieces = [shared] + [part.reshape(-1) for part in own]
    count = sum(piece.size for piece in pieces)
    total = -(-count // 2048) * 2048
    small = jnp.concatenate(pieces + [jnp.zeros((total - count,), F32)]).reshape(-1, 128)
    x_part, bc_part, small, out_proj_grad, z_proj_grad = lax.optimization_barrier(
        (x_proj_part.astype(BF16), bc_proj_part, small.astype(BF16), out_proj_grad, z_proj_grad)
    )
    x_proj_grad, bc_proj_grad, small = lax.psum((x_part, bc_part, small), "dp")

    summed = nt(z_low, z_proj) + nt(x_low, x_proj) + nt(dt_low, dt_proj) + nt(bc_low, bc_proj)
    full_grad = over_tensor(summed.astype(BF16)).astype(F32)
    scaled = full_grad * norm_gain
    full_back = inv_rms * (scaled - normed * jnp.mean(scaled * normed, axis=1, keepdims=True))
    tokens_grad = (full_back + cotangent.astype(F32)).astype(BF16)

    flat = small.reshape(-1).astype(F32)
    taken = []
    start = 0
    shapes = [(width,), bc_conv.shape, bc_conv_bias.shape] + [part.shape for part in own]
    for shape in shapes:
        size = 1
        for dim in shape:
            size *= dim
        taken.append(flat[start : start + size].reshape(shape))
        start += size
    (
        norm_gain_grad, bc_conv_grad, bc_conv_bias_grad, dt_proj_grad, x_conv_grad,
        x_conv_bias_grad, dt_bias_grad, a_log_grad, d_skip_grad, gate_gain_grad,
    ) = taken
    return (
        mixed,
        tokens_grad,
        norm_gain_grad,
        z_proj_grad.astype(F32),
        x_proj_grad.astype(F32),
        dt_proj_grad,
        bc_proj_grad.astype(F32),
        x_conv_grad,
        x_conv_bias_grad,
        bc_conv_grad,
        bc_conv_bias_grad,
        dt_bias_grad,
        a_log_grad,
        d_skip_grad,
        gate_gain_grad,
        out_proj_grad.astype(F32),
    )


def solution(mesh):
    placed = (
        P("dp", None),
        P(),
        P(None, "tensor"),
        P(None, "tensor"),
        P(None, "tensor"),
        P(),
        P(None, "tensor"),
        P("tensor"),
        P(),
        P(),
        P("tensor"),
        P("tensor"),
        P("tensor"),
        P("tensor"),
        P("tensor", None),
        P("dp", None),
    )
    return jax.shard_map(
        per_device,
        mesh=mesh,
        in_specs=placed,
        out_specs=(
            P("dp", None),
            P("dp", None),
            P(),
            P(None, "tensor"),
            P(None, "tensor"),
            P(None, "tensor"),
            P(),
            P(None, "tensor"),
            P("tensor"),
            P(),
            P(),
            P("tensor"),
            P("tensor"),
            P("tensor"),
            P("tensor"),
            P("tensor", None),
        ),
        check_vma=False,
    )
```

time: 843 us -> 487 us (0.58)
  matrix products: 221 us -> 54.7 us
  other arithmetic: 121 us -> 34.6 us
  local copies, waits for them, and re-layouts: 125 us -> 57.4 us
  blocking collectives: 125 us -> 76.4 us
  Pallas kernels: 0 us -> 48.3 us
  waiting for transfers between devices: 227 us -> 193 us
    dot_general x71 -> x17, matrix products: 221 us -> 54.7 us  [the longest x5 22.7 us: nt(): lax.dot_general(left, right, (((1,), (1,)), ((), ())), preferred_element_...]
    psum x4 -> x1, blocking collectives: 125 us -> 76.4 us  [per_device(): x_proj_grad, bc_proj_grad, small = lax.psum((x_part, bc_part, small), 'dp')]
    pallas_call x0 -> x2, Pallas kernels: none -> 48.3 us  [the longest x1 31.9 us: scan_backward(): pl.pallas_call(backward_kernel, grid=(groups,), in_specs=[wide(), wide(),...]
    psum x3 -> x2, waiting for transfers between devices: 227 us -> 192 us  [the longest x1 146 us: per_device(): lax.psum((out_proj_grad, z_proj_part.astype(BF16)), 'dp')]
    another operation x40 -> x3, other arithmetic: 30.8 us -> 0.02 us
    transpose x4, local copies, waits for them, and re-layouts: 31.8 us -> 6.93 us  [the longest x2 6.07 us: from_groups(): return pairs.transpose(1, 0, 2).reshape(rows, groups * 2)]
    squeeze x16 -> x0, local copies, waits for them, and re-layouts: 22.5 us -> none  [ssd_sequence(): lax.scan(jax.checkpoint(advance), initial, (values.reshape(block_count, S...]
    mul x18 -> x0, other arithmetic: 18.1 us -> none  [the longest x4 5.99 us: advance(): jnp.exp(cumulative[-1])[:, None, None]]
  transfers between devices with their start and end apart: 3 -> 7, of which waited for: 2 -> 3; matrix products, arithmetic and copies ran while one was open for 5% -> 11% of each run, Pallas kernels for 0% -> 0%
where the time goes in v1:
time: 487 us; the launch traced here: 481 us
  waiting for transfers between devices  193 us (40%)
  blocking collectives  76.4 us (16%)
  local copies, waits for them, and re-layouts  57.4 us (12%)
  matrix products  54.7 us (11%)
  Pallas kernels  48.3 us (10%)
  other arithmetic  34.6 us (7%)
  between operations  14.9 us (3%)
    psum x1, waiting for transfers between devices, per_device(): lax.psum((out_proj_grad, z_proj_part.astype(BF16)), 'dp')  146 us
    psum x1, blocking collectives, per_device(): x_proj_grad, bc_proj_grad, small = lax.psum((x_part, bc_part, small), 'dp')  76.4 us
    psum x1, waiting for transfers between devices, per_device(): x_proj_grad, bc_proj_grad, small = lax.psum((x_part, bc_part, small), 'dp')  46.3 us
    unnamed x122, local copies, waits for them, and re-layouts  37.4 us
    pallas_call x1, Pallas kernels, scan_backward(): pl.pallas_call(backward_kernel, grid=(groups,), in_specs=[wide(), wide(),...  31.9 us
    dot_general x5, matrix products, nt(): lax.dot_general(left, right, (((1,), (1,)), ((), ())), preferred_element_...  22.7 us
    pallas_call x1, Pallas kernels, scan_forward(): pl.pallas_call(forward_kernel, grid=(groups,), in_specs=[wide(), wide(),...  16.4 us
    dot_general x5, matrix products, nn(): return jnp.dot(left, right, preferred_element_type=F32)  16 us
  transfers between devices with their start and end apart: 7, of which 3 were waited for; matrix products, arithmetic and copies ran while one was open for 11% of the time, Pallas kernels for 0%

profile of v1, /device:TPU:0, one launch (start us, length us, event | category | flops | bytes accessed | tf_op | source)
XLA Modules:
  0.0 480.8 jit_solution(15700985547065676597)
XLA Ops:
  7.3 2.2 fusion.9
  11.4 1.6 copy-done.33
  13.0 4.4 fusion.38.x_ref
  17.4 4.4 fusion.39.z_ref
  21.8 2.1 fusion.18
  25.2 2.9 broadcast_multiply_fusion.4
  28.1 2.9 copy.115
  31.4 2.7 copy.118
  34.3 4.1 fusion.40.gi_ref
  38.5 16.4 %shard_map.279 = (f32[1024,1024]{1,0:T(8,128)S(1)}, f32[8,4,128,128]{3,2,1,0:T(8,128)S(1)}, f32[1024,2]{1,0:T(8,128)S(1)}) custom-call(f32[1024,1024]{1,0:T(8,128)S(1)} %copy-done.7, f32[1024,1024]{1,0:T(8,128)S(1)} %copy-done.1, f32[1024,1024]{1,0:T(8,128)S(1)} %fusion.40.gi_ref, bf16[1024,128]{1,0:T(8,128)(2,1)S(1)} %copy.120.b_ref, ...), custom_call_target="tpu_custom_call" | custom-call | flops 2000000000 | bytes 25165824 | tf_op jit(solution)/shard_map/pallas_call | solution.py:262
  54.9 1.9 copy-done.5
  56.9 1.3 copy-done.16
  58.6 4.0 copy.135
  62.6 2.0 copy.136
  64.6 3.9 copy.134
  68.6 1.3 add.138
  71.2 1.6 copy-done.17
  72.7 31.9 %shard_map.280 = (bf16[1024,1024]{1,0:T(8,128)(2,1)S(1)}, f32[8,1024,2]{2,1,0:T(8,128)S(1)}, f32[8,1024,2]{2,1,0:T(8,128)S(1)}, f32[8,1024]{1,0:T(8,128)S(1)}, f...) custom-call(f32[1024,1024]{1,0:T(8,128)S(1)} %copy-done.8, f32[1024,1024]{1,0:T(8,128)} %fusion.39.z_ref, ...), custom_call_target="tpu_custom_call" | custom-call | flops 60000002048 | bytes 209715200 | tf_op jit(solution)/shard_map/pallas_call | solution.py:295
  104.7 2.0 copy-done.9
  106.7 2.0 copy-done.10
  109.5 1.3 copy-done.18
  110.8 1.2 copy.132
  112.0 1.0 copy.131
  113.0 4.4 multiply_reduce_fusion.6
  117.8 0.9 fusion.14
  119.0 2.9 fusion.44
  121.9 2.0 copy-done.2
  124.0 1.9 multiply_reduce_fusion
  125.9 3.8 convolution_convert_fusion
  129.7 2.6 multiply_convert_fusion
  132.3 4.4 fusion.42
  136.7 4.4 fusion.43
  141.1 3.2 copy.129
  144.4 2.8 copy.126
  147.6 6.7 %fusion.34 = (bf16[1024,1024]{0,1:T(8,128)(2,1)}, f32[1024]{0:T(1024)S(1)}) fusion(bf16[1024,1024]{0,1:T(8,128)(2,1)} %copy.134, bf16[1024,1024]{1,0:T(8,128)(2,1)} %copy-done.22, bf16[1024,1024]{1,0:T(8,128)(2,1)} %copy-done.30), kind=kOutput, calls=%fused_computation.95 | convolution fusion | flops 2151676928 | bytes 8392704 | tf_op jit(solution)/shard_map/dot_general | solution.py:39
  155.3 6.9 %add_convert_fusion = bf16[1024,1024]{1,0:T(8,128)(2,1)} fusion(f32[1024,1024]{1,0:T(8,128)} %fusion.44, f32[1024,1024]{1,0:T(8,128)} %fusion.42, f32[1024,1024]{1,0:T(8,128)} %fusion.43, bf16[1024,16]{0,1:T(8,128)(2,1)S(1)} %copy-done.39, bf16[1024,16]{0,1:T(8,128)(2,1)S(1)} %get-tuple-element.123), kind=kOutput, calls=%fused_computation.18 | convolution fusion | flops 37748736 | bytes 14745600 | tf_op jit(solution)/shard_map/dot_general | solution.py:35
  162.3 3.7 convolution_convert_fusion.1
  167.6 3.8 multiply_reduce_fusion.1
  173.5 2.0 add.150
  175.5 4.1 fusion.4
  179.6 146.1 %all-reduce.16.cloned.1.call-done = (bf16[1024,1024]{1,0:T(8,128)(2,1)}, bf16[1024,1024]{0,1:T(8,128)(2,1)}) async-done(((bf16[1024,1024]{1,0:T(8,128)(2,1)}, bf16[1024,1024]{0,1:T(8,128)(2,1)}), (bf16[1024,1024]{1,0:T(8,128)(2,1)}, bf16[1024,1024]{0,1:T(8,128)(2,1)})) %all-reduce.16.cloned.1.call-update) | async-done | bytes 4194320 | tf_op jit(solution)/shard_map/psum | solution.py:386
  325.8 7.1 %fusion.8 = (bf16[1024,1024]{1,0:T(8,128)(2,1)}, bf16[1024,1024]{1,0:T(8,128)(2,1)}) fusion(bf16[1024,1024]{1,0:T(8,128)(2,1)} %param.16, bf16[1024,1024]{1,0:T(8,128)(2,1)} %param.31, f32[1024]{0:T(1024)S(1)} %broadcast_multiply_fusion.5, f32[1024]{0:T(1024)S(1)} %copy-done.41, f32[1024]{0:T(1024)S(1)} %add_rsqrt_fusion, ...), kind=kLoop, calls=%fused_computation.11 | loop fusion | flops 15728640 | bytes 16789504 | tf_op jit(solution)/shard_map/convert_element_type | solution.py:434
  332.9 4.1 copy.138
  337.0 76.4 %psum.37 = bf16[208,128]{1,0:T(8,128)(2,1)S(1)} all-reduce(bf16[208,128]{1,0:T(8,128)(2,1)S(1)} %bitcast.119), channel_id=1, replica_groups=mesh['dp'=16,'tensor'=2] {'dp'}, use_global_device_ids=true, to_apply=%region_17.18 | all-reduce | flops 26624 | bytes 106496 | tf_op jit(solution)/shard_map/psum | solution.py:428
  416.3 4.1 convert_element_type.128
  422.1 46.3 %all-reduce.14.cloned.1.call-done = (bf16[1024,1024]{0,1:T(8,128)(2,1)}, bf16[1024,256]{0,1:T(8,128)(2,1)}) async-done(((bf16[1024,1024]{0,1:T(8,128)(2,1)}, bf16[1024,256]{0,1:T(8,128)(2,1)}), (bf16[1024,1024]{0,1:T(8,128)(2,1)}, bf16[1024,256]{0,1:T(8,128)(2,1)})) %all-reduce.14.cloned.1.call-update) | async-done | bytes 2621456 | tf_op jit(solution)/shard_map/psum | solution.py:428
  468.4 4.2 copy.139
  472.6 1.2 copy.141
  (174 shorter events, 16.7 us)
Async XLA Ops:
  7.2 27.1 %copy-start = (bf16[1024,1024]{1,0:T(8,128)(2,1)S(1)}, bf16[1024,1024]{1,0:T(8,128)(2,1)}, u32[]{:S(2)}) copy-start(bf16[1024,1024]{1,0:T(8,128)(2,1)} %param.30) | copy-start | bytes 6291460
  7.2 2.3 copy-start.48
  7.2 2.3 copy-start.41
  7.2 318.5 %all-reduce.16.cloned.1.call-start = ((), (), s32[]{:S(2)}) async-start(), calls=%async_computation.1 | async-start | bytes 8388608 | tf_op jit(solution)/shard_map/psum | solution.py:386
  7.3 2.3 copy-start.21
  9.6 12.1 %copy-start.42 = (f32[1,256]{1,0:T(1,128)}, f32[1,256]{1,0:T(1,128)S(1)}, u32[]{:S(2)}) copy-start(f32[1,256]{1,0:T(1,128)S(1)} %get-tuple-element.162) | copy-start | bytes 3076
  9.6 12.1 %copy-start.44 = (f32[1,256]{1,0:T(1,128)}, f32[1,256]{1,0:T(1,128)S(1)}, u32[]{:S(2)}) copy-start(f32[1,256]{1,0:T(1,128)S(1)} %get-tuple-element.163) | copy-start | bytes 3076
  9.6 12.1 %copy-start.46 = (f32[1,256]{1,0:T(1,128)}, f32[1,256]{1,0:T(1,128)S(1)}, u32[]{:S(2)}) copy-start(f32[1,256]{1,0:T(1,128)S(1)} %get-tuple-element.164) | copy-start | bytes 3076
  10.7 6.7 %copy-start.22 = (bf16[1024,1024]{1,0:T(8,128)(2,1)}, bf16[1024,1024]{1,0:T(8,128)(2,1)S(1)}, u32[]{:S(2)}) copy-start(bf16[1024,1024]{1,0:T(8,128)(2,1)S(1)} %fusion.3) | copy-start | bytes 6291460
  10.7 2.3 copy-start.33
  13.0 8.8 %copy-start.24 = (f32[1024,256]{0,1:T(8,128)}, f32[1024,256]{0,1:T(8,128)S(1)}, u32[]{:S(2)}) copy-start(f32[1024,256]{0,1:T(8,128)S(1)} %fusion.41) | copy-start | bytes 3145732
  13.0 4.4 copy-start.31
  17.4 4.4 copy-start.51
  25.1 5.8 %copy-start.49 = (f32[16]{0:T(128)}, f32[16]{0:T(128)S(1)}, u32[]{:S(2)}) copy-start(f32[16]{0:T(128)S(1)} %exponential_negate_fusion) | copy-start | bytes 196
  31.4 2.7 copy-start.52
  34.3 4.2 copy-start.1
  34.3 4.2 copy-start.7
  34.3 4.2 copy-start.13
  34.3 4.2 copy-start.14
  34.3 4.2 copy-start.15
  38.4 16.5 %copy-start.3 = (f32[1024,1024]{1,0:T(8,128)}, f32[1024,1024]{1,0:T(8,128)S(1)}, u32[]{:S(2)}) copy-start(f32[1024,1024]{1,0:T(8,128)S(1)} %fusion.40.gi_ref) | copy-start | bytes 12582916
  54.9 1.9 copy-start.5
  58.2 10.4 %collective-permute-start = (f32[1024,2]{1,0:T(8,128)S(1)}, f32[1024,2]{1,0:T(8,128)}, u32[]{:S(2)}, u32[]{:S(2)}) collective-permute-start(f32[1024,2]{1,0:T(8,128)S(1)} %get-tuple-element.31), channel_id=1, source_target_pairs={{0,1},{1,0},{2,3},{3,2},{4,5},{5,4},{6,7},{7,6},{8,9},{9,8},{10,11... | collective-permute-start | bytes 24584 | tf_op jit(solution)/shard_map/ppermute | solution.py:332
  68.6 2.3 copy-start.8
  104.7 2.0 copy-start.9
  106.7 2.0 copy-start.10
  113.0 4.4 copy-start.43
  113.0 4.4 copy-start.45
  113.0 4.4 copy-start.47
  117.4 4.5 copy-start.6
  117.8 4.1 copy-start.4
  119.0 4.9 %copy-start.2 = (f32[1024,1024]{1,0:T(8,128)S(1)}, f32[1024,1024]{1,0:T(8,128)}, u32[]{:S(2)}) copy-start(f32[1024,1024]{1,0:T(8,128)} %fusion.39.z_ref) | copy-start | bytes 12582916
  124.0 1.9 copy-start.29
  125.9 3.8 copy-start.25
  129.7 2.6 copy-start.32
  132.3 4.4 copy-start.30
  132.3 4.4 copy-start.19
  132.3 4.4 copy-start.34
  154.3 314.1 %all-reduce.14.cloned.1.call-start = ((), (), s32[]{:S(2)}) async-start(), calls=%async_computation | async-start | bytes 5242880 | tf_op jit(solution)/shard_map/psum | solution.py:428
  155.3 7.0 %copy-start.26 = (f32[1024,1024]{1,0:T(8,128)S(1)}, f32[1024,1024]{1,0:T(8,128)}, u32[]{:S(2)}) copy-start(f32[1024,1024]{1,0:T(8,128)} %copy-done.25) | copy-start | bytes 12582916
  162.3 4.2 copy-start.23
  162.3 4.2 copy-start.37
  162.3 13.3 %collective-permute-start.2 = (bf16[1024,1024]{1,0:T(8,128)(2,1)}, bf16[1024,1024]{1,0:T(8,128)(2,1)}, u32[]{:S(2)}, u32[]{:S(2)}) collective-permute-start(bf16[1024,1024]{1,0:T(8,128)(2,1)} %add_convert_fusion), channel_id=1, source_target_pairs={{0,1},{1,0},{2,3},{3,2},{4,5},{5,4},{6,7},{7,6},{8,9},{9,8},{10,11... | collective-permute-start | bytes 6291464 | tf_op jit(solution)/shard_map/ppermute | solution.py:332
  162.3 5.0 %copy-start.35 = (bf16[1024,1024]{0,1:T(8,128)(2,1)S(1)}, bf16[1024,1024]{0,1:T(8,128)(2,1)}, u32[]{:S(2)}) copy-start(bf16[1024,1024]{0,1:T(8,128)(2,1)} %copy.135) | copy-start | bytes 6291460
  166.0 159.8 %collective-permute-start.1 = (bf16[1024,1024]{1,0:T(8,128)(2,1)}, bf16[1024,1024]{1,0:T(8,128)(2,1)}, u32[]{:S(2)}, u32[]{:S(2)}) collective-permute-start(bf16[1024,1024]{1,0:T(8,128)(2,1)} %convolution_convert_fusion.1), channel_id=1, source_target_pairs={{0,1},{1,0},{2,3},{3,2},{4,5},{5,4},{6,7},{7,6},{8,9},{9,8},{10,11... | collective-permute-start | bytes 6291464 | tf_op jit(solution)/shard_map/ppermute | solution.py:332
  167.2 6.3 %collective-permute-start.3 = (bf16[1024,256]{0,1:T(8,128)(2,1)S(1)}, bf16[1024,256]{0,1:T(8,128)(2,1)}, u32[]{:S(2)}, u32[]{:S(2)}) collective-permute-start(bf16[1024,256]{0,1:T(8,128)(2,1)S(1)} %get-tuple-element.136), channel_id=1, source_target_pairs={{0,1},{1,0},{2,3},{3,2},{4,5},{5,4},{6,7},{7,6},{8,9},{9,8},{10,11... | collective-permute-start | bytes 1572872 | tf_op jit(solution)/shard_map/ppermute | solution.py:332
  171.8 1.4 collective-permute-start.4
  468.4 4.2 copy-start.36
  (15 other events, 17.5 us)
Sparse Core Ops, SparseCore 0:
  154.4 171.2 all-reduce.15
  332.7 135.6 all-reduce.13
